TPU v7x, 32 devices: a whole 2x2x4 slice. The times are simulated.
32 devices in a mesh: mask: 4 (over z), rows: 8 (over y, x, core).
Axes of the slice: x: 2, y: 2, z: 4, core: 2. Of those that a mesh axis runs over, the one named last changes fastest.
Arguments:
- object_field: float32 [2, 4096, 4096], P(None, 'rows'), may hold values from -6 to 6
- phases: int32 [4, 4096, 4096], P('mask', 'rows'), may hold values from 0 to 3
- intensity: float32 [4, 4096, 4096], P('mask', 'rows'), may hold values from 0.5 to 4
Outputs:
- updated: float32 [2, 4096, 4096], P(None, 'rows')
- gradient: float32 [2, 4096, 4096], P(None, 'rows')
Inputs may be any that keep to these rules, and one draw needn't show every extreme that they name: `phases`: index k stands for the mask entry i^k.
All inputs are finite; a program needn't handle non-finite values.
Results may differ from a plain program's by a relative error of at most 0.00011.
Values sent between devices are 32-bit elements; how exact they have to be, the bound alone decides.
A program may use at most 192 MiB of HBM per device.

v0:
```python
import math

import jax
import jax.numpy as jnp
from jax import lax
from jax.sharding import PartitionSpec as P

P_SIZE = 32
Q = 128


step_size = 0.2


def dft_table(length, sign):
    idx = jnp.arange(length, dtype=jnp.int32)
    expo = idx[:, None] * idx[None, :] % length
    angle = expo.astype(jnp.float32) * (sign * 2.0 * math.pi / length)
    return (jnp.cos(angle), jnp.sin(angle))


def twiddle_table(first, second, sign):
    left = jnp.arange(first, dtype=jnp.int32)
    right = jnp.arange(second, dtype=jnp.int32)
    total = first * second
    expo = left[:, None] * right[None, :] % total
    angle = expo.astype(jnp.float32) * (sign * 2.0 * math.pi / total)
    return (jnp.cos(angle), jnp.sin(angle))


def stacked_table(t_real, t_imag):
    upper = jnp.stack([t_real, t_imag], axis=1)
    lower = jnp.stack([-t_imag, t_real], axis=1)
    return jnp.stack([upper, lower])


def contract(form, left, right):
    return jnp.einsum(
        form, left, right, precision=lax.Precision.HIGHEST, preferred_element_type=jnp.float32
    )


def along_last(stacked, sign, flip):
    lead = stacked.shape[1]
    length = P_SIZE * Q
    p_real, p_imag = dft_table(P_SIZE, sign)
    q_real, q_imag = dft_table(Q, sign)
    t_real, t_imag = twiddle_table(P_SIZE, Q, sign)
    factor = 1.0 / math.sqrt(length)
    first_table = stacked_table(p_real, p_imag)
    second_table = stacked_table(q_real * factor, q_imag * factor)
    inner = contract("cbpq,cpek->ebkq", stacked.reshape(2, lead, P_SIZE, Q), first_table)
    b_real = inner[0] * t_real - inner[1] * t_imag
    b_imag = inner[0] * t_imag + inner[1] * t_real
    twisted = jnp.stack([b_real, b_imag])
    if flip:
        return contract("cbkq,cqem->emkb", twisted, second_table).reshape(2, length, lead)
    return contract("cbkq,cqem->ebmk", twisted, second_table).reshape(2, lead, length)


def body(object_field, phases, intensity):
    groups = lax.axis_size("rows")
    masks = lax.axis_size("mask")
    own_rows = object_field.shape[1]
    length = object_field.shape[2]
    own_cols = length // groups
    code = phases[0]
    d_real = jnp.where(code == 0, 1.0, 0.0) - jnp.where(code == 2, 1.0, 0.0)
    d_imag = jnp.where(code == 1, 1.0, 0.0) - jnp.where(code == 3, 1.0, 0.0)
    z_real = object_field[0]
    z_imag = object_field[1]
    coded = jnp.stack([d_real * z_real - d_imag * z_imag, d_real * z_imag + d_imag * z_real])
    result = along_last(coded, -1.0, True)
    received = lax.all_to_all(
        result.reshape(2, groups, own_cols, own_rows),
        "rows",
        split_axis=1,
        concat_axis=1,
        tiled=True,
    )
    columns = jnp.transpose(received, (0, 2, 1, 3)).reshape(2, own_cols, length)
    wave = along_last(columns, -1.0, False)
    weight = wave[0] * wave[0] + wave[1] * wave[1] - intensity[0]
    weighted = along_last(wave * weight[None], 1.0, False)
    outgoing = weighted.reshape(2, own_cols, groups, own_rows)
    returned = lax.all_to_all(outgoing, "rows", split_axis=2, concat_axis=2, tiled=True)
    panel = jnp.transpose(returned, (0, 3, 2, 1)).reshape(2, own_rows, length)
    back = along_last(panel, 1.0, False)
    g_real = back[0]
    g_imag = back[1]
    term = jnp.stack([d_real * g_real + d_imag * g_imag, d_real * g_imag - d_imag * g_real])
    inverse_count = 1.0 / masks
    total = lax.psum(term, "mask")
    direction = inverse_count * total
    return (object_field - step_size * direction, direction)


def solution(mesh):
    return jax.shard_map(
        body,
        mesh=mesh,
        in_specs=(P(None, "rows", None), P("mask", "rows", None), P("mask", "rows", None)),
        out_specs=(P(None, "rows", None), P(None, "rows", None)),
        check_vma=False,
    )
```

profile of v0, /device:TPU:0, one launch (start us, length us, event | category | flops | bytes accessed | tf_op | source)
XLA Modules:
  0.0 1611.3 jit_solution(15460839452836750417)
XLA Ops:
  8.0 17.5 %copy.76 = f32[2,512,4096]{1,2,0:T(8,128)} copy(f32[2,512,4096]{2,1,0:T(8,128)} %param.3) | data formatting | bytes 33554432 | tf_op args[0]
  34.4 16.8 %multiply_subtract_fusion.5 = (f32[1,512,4096]{1,2,0:T(8,128)}, pred[1,512,4096]{1,2,0:T(8,128)(4,1)S(1)}, pred[1,512,4096]{1,2,0:T(8,128)(4,1)S(1)}, pred[1,512,4096]{1,2,0:T(8,128)(4,1)}, pred[1,512,4096]{1,2,0:T(8,128)(4,1)}) fusion(f32[2,512,4096]{1,2,0:T(8,128)} %copy.76, s32[1,512,4096]{1,2,0:T(8,128)} %copy.46), kind=kLoop, calls=%fused_computation.45 | loop fusion | flops 27262976 | bytes 41943040 | tf_op jit(solution)/shard_map/sub | solution.py:72
  81.6 22.6 %fusion.35 = f32[2,512,32,128]{3,2,1,0:T(8,128)} fusion(f32[1,512,32,128]{3,2,0,1:T(8,128)} %copy.102, f32[1,512,32,128]{3,2,0,1:T(8,128)} %copy.101, f32[1,32,2,32]{1,3,0,2:T(8,128)S(1)} %get-tuple-element.32, f32[1,32,2,32]{1,3,0,2:T(8,128)S(1)} %get-tuple-element.31), kind=kOutput, calls=%fused_computation.53 | convolution fusion | flops 3225423872 | bytes 33570816 | tf_op jit(solution)/shard_map/cbpq,cpek->ebkq/dot_general | solution.py:38
  117.8 32.8 %fusion.20 = f32[2,128,32,512]{3,1,2,0:T(8,128)} fusion(f32[2,512,32,128]{3,2,1,0:T(8,128)} %pad_maximum_fusion, f32[1,128,2,128]{1,3,0,2:T(8,128)S(1)} %get-tuple-element.28, f32[1,128,2,128]{1,3,0,2:T(8,128)S(1)} %get-tuple-element.27), kind=kOutput, calls=%fused_computation.48 | convolution fusion | flops 12884967424 | bytes 33816576 | tf_op jit(solution)/shard_map/cbkq,cqem->emkb/dot_general | solution.py:38
  150.6 15.3 copy.57
  187.9 174.7 %all-to-all-done = f32[2,8,512,512]{3,2,0,1:T(8,128)} async-done(((f32[2,8,512,512]{3,2,0,1:T(8,128)}), f32[2,8,512,512]{3,2,0,1:T(8,128)}, u32[]{:S(2)}, u32[]{:S(2)}) %all-to-all-start) | async-done | bytes 16777248 | tf_op jit(solution)/shard_map/all_to_all | solution.py:74
  362.6 17.8 %copy.59 = f32[2,512,8,512]{3,2,0,1:T(8,128)} copy(f32[2,512,8,512]{3,1,0,2:T(8,128)} %bitcast.32) | data formatting | bytes 33554432 | tf_op jit(solution)/shard_map/transpose | solution.py:81
  380.3 17.4 %reshape.339 = f32[2,512,32,128,1]{3,2,0,1,4:T(8,128)} reshape(f32[2,512,8,512]{3,2,0,1:T(8,128)} %copy.59) | data formatting | bytes 33554432 | tf_op jit(solution)/shard_map/reshape;reshape | solution.py:52
  397.7 22.5 %convolution_bitcast_fusion.1 = f32[2,512,32,128]{3,2,1,0:T(8,128)} fusion(f32[2,512,32,128,1]{3,2,0,1,4:T(8,128)} %reshape.339, f32[1,32,2,32]{1,3,0,2:T(8,128)S(1)} %get-tuple-element.32, f32[1,32,2,32]{1,3,0,2:T(8,128)S(1)} %get-tuple-element.31), kind=kOutput, calls=%fused_computation.55 | convolution fusion | flops 3221229568 | bytes 33570816 | tf_op jit(solution)/shard_map/cbpq,cpek->ebkq/dot_general | solution.py:38
  433.7 32.8 %fusion.23 = f32[2,512,128,32]{1,2,3,0:T(8,128)} fusion(f32[2,512,32,128]{3,2,1,0:T(8,128)} %pad_maximum_fusion.1, f32[1,128,2,128]{1,3,0,2:T(8,128)S(1)} %get-tuple-element.28, f32[1,128,2,128]{1,3,0,2:T(8,128)S(1)} %get-tuple-element.27), kind=kOutput, calls=%fused_computation.49 | convolution fusion | flops 12884967424 | bytes 33816576 | tf_op jit(solution)/shard_map/cbkq,cqem->ebmk/dot_general | solution.py:38
  477.2 20.0 %copy.61 = f32[2,512,128,32]{1,3,2,0:T(8,128)} copy(f32[2,512,128,32]{1,2,3,0:T(8,128)S(1)} %copy-done.1) | data formatting | bytes 33554432 | tf_op jit(solution)/shard_map/cbkq,cqem->ebmk/transpose | solution.py:38
  530.8 19.9 %copy.65 = f32[2,512,32,128]{3,2,0,1:T(8,128)} copy(f32[2,512,32,128]{1,3,2,0:T(8,128)} %bitcast_multiply_fusion) | data formatting | bytes 33554432 | tf_op jit(solution)/shard_map/mul | solution.py:84
  550.7 22.7 %fusion.26 = f32[2,512,32,128]{3,2,1,0:T(8,128)} fusion(f32[2,512,32,128]{3,2,0,1:T(8,128)} %copy.65, f32[1,32,2,32]{1,3,2,0:T(8,128)S(1)} %get-tuple-element.30, f32[1,32,2,32]{1,3,2,0:T(8,128)S(1)} %get-tuple-element.29), kind=kOutput, calls=%fused_computation.50 | convolution fusion | flops 3221229568 | bytes 33570816 | tf_op jit(solution)/shard_map/cbpq,cpek->ebkq/dot_general | solution.py:38
  586.9 32.6 %fusion.29 = f32[2,512,128,32]{1,2,3,0:T(8,128)} fusion(f32[2,512,32,128]{3,2,1,0:T(8,128)} %pad_maximum_fusion.2, f32[1,128,2,128]{1,3,2,0:T(8,128)S(1)} %get-tuple-element.26, f32[1,128,2,128]{1,3,2,0:T(8,128)S(1)} %get-tuple-element.25), kind=kOutput, calls=%fused_computation.51 | convolution fusion | flops 12884967424 | bytes 33816576 | tf_op jit(solution)/shard_map/cbkq,cqem->ebmk/dot_general | solution.py:38
  619.5 15.3 copy.68
  636.7 186.6 %all_to_all.10 = f32[2,512,8,512]{1,3,0,2:T(8,128)S(1)} all-to-all(f32[2,512,8,512]{1,3,0,2:T(8,128)S(1)} %copy.69), channel_id=1, replica_groups=mesh['mask'=4,'rows'=8] {'rows'}, dimensions={2} | all-to-all | bytes 33554432 | tf_op jit(solution)/shard_map/all_to_all | solution.py:86
  823.3 21.0 %copy.70 = f32[2,512,8,512]{3,2,0,1:T(8,128)} copy(f32[2,512,8,512]{3,1,0,2:T(8,128)S(1)} %bitcast.155) | data formatting | bytes 33554432 | tf_op jit(solution)/shard_map/transpose | solution.py:87
  844.3 17.4 %reshape.350 = f32[2,512,32,128,1]{3,2,0,1,4:T(8,128)} reshape(f32[2,512,8,512]{3,2,0,1:T(8,128)} %copy.70) | data formatting | bytes 33554432 | tf_op jit(solution)/shard_map/reshape;reshape | solution.py:52
  861.7 22.7 %convolution_bitcast_fusion = f32[2,512,32,128]{3,2,1,0:T(8,128)} fusion(f32[2,512,32,128,1]{3,2,0,1,4:T(8,128)} %reshape.350, f32[1,32,2,32]{1,3,2,0:T(8,128)S(1)} %get-tuple-element.30, f32[1,32,2,32]{1,3,2,0:T(8,128)S(1)} %get-tuple-element.29), kind=kOutput, calls=%fused_computation.54 | convolution fusion | flops 3221229568 | bytes 33570816 | tf_op jit(solution)/shard_map/cbpq,cpek->ebkq/dot_general | solution.py:38
  897.9 32.6 %fusion.32 = f32[2,512,128,32]{1,2,3,0:T(8,128)} fusion(f32[2,512,32,128]{3,2,1,0:T(8,128)} %pad_maximum_fusion.3, f32[1,128,2,128]{1,3,2,0:T(8,128)S(1)} %get-tuple-element.26, f32[1,128,2,128]{1,3,2,0:T(8,128)S(1)} %get-tuple-element.25), kind=kOutput, calls=%fused_computation.52 | convolution fusion | flops 12884967424 | bytes 33816576 | tf_op jit(solution)/shard_map/cbkq,cqem->ebmk/dot_general | solution.py:38
  985.1 562.5 %all-reduce.2.cloned.1.call-done = f32[2,512,4096]{1,2,0:T(8,128)} async-done(((f32[2,512,4096]{1,2,0:T(8,128)}), f32[2,512,4096]{1,2,0:T(8,128)}) %all-reduce.2.cloned.1.call-update) | async-done | bytes 16777232 | tf_op jit(solution)/shard_map/psum | solution.py:93
  1547.6 21.5 %broadcast_multiply_fusion = (f32[2,512,4096]{1,2,0:T(8,128)}, f32[2,512,4096]{1,2,0:T(8,128)}) fusion(f32[2,512,4096]{1,2,0:T(8,128)} %all-reduce.2.cloned.1.call-done, f32[2,512,4096]{1,2,0:T(8,128)} %copy.76), kind=kLoop, calls=%fused_computation.35 | loop fusion | flops 12582912 | bytes 67108864 | tf_op jit(solution)/shard_map/mul | solution.py:94
  1569.1 17.5 %copy.77 = f32[2,512,4096]{2,1,0:T(8,128)} copy(f32[2,512,4096]{1,2,0:T(8,128)} %get-tuple-element.22) | data formatting | bytes 33554432
  1586.6 17.5 %copy.78 = f32[2,512,4096]{2,1,0:T(8,128)} copy(f32[2,512,4096]{1,2,0:T(8,128)} %get-tuple-element.21) | data formatting | bytes 33554432
  (53 shorter events, 216.8 us)
Async XLA Ops:
  34.4 16.8 %copy-start = (f32[2,512,4096]{1,2,0:T(8,128)S(1)}, f32[2,512,4096]{1,2,0:T(8,128)}, u32[]{:S(2)}) copy-start(f32[2,512,4096]{1,2,0:T(8,128)} %copy.76) | copy-start | bytes 50331652
  51.2 9.8 copy-start.2
  51.2 9.8 copy-start.4
  172.2 190.3 %all-to-all-start = ((f32[2,8,512,512]{3,2,0,1:T(8,128)}), f32[2,8,512,512]{3,2,0,1:T(8,128)}, u32[]{:S(2)}, u32[]{:S(2)}) async-start(f32[2,8,512,512]{3,2,0,1:T(8,128)} %copy.58), calls=%async_computation | async-start | bytes 33554432 | tf_op jit(solution)/shard_map/all_to_all | solution.py:74
  178.0 1369.7 %all-reduce.2.cloned.1.call-start = ((), (), s32[]{:S(2)}) async-start(), calls=%async_computation.2 | async-start | bytes 33554432 | tf_op jit(solution)/shard_map/psum | solution.py:93
  466.6 10.6 copy-start.1
  949.8 11.8 copy-start.3
  949.8 11.8 copy-start.5
Sparse Core Ops, SparseCore 0:
  985.2 562.3 all-reduce.1
where the time goes:
time: 1620 us; the launch traced here: 1610 us
  waiting for transfers between devices  737 us (45%)
  local copies, waits for them, and re-layouts  286 us (18%)
  matrix products  221 us (14%)
  blocking collectives  187 us (12%)
  other arithmetic  160 us (10%)
    psum x1, waiting for transfers between devices, body(): total = lax.psum(term, 'mask')  563 us
    dot_general x8, matrix products, contract(): jnp.einsum(form, left, right, precision=lax.Precision.HIGHEST, preferred_...  221 us
    all_to_all x1, blocking collectives, body(): lax.all_to_all(outgoing, 'rows', split_axis=2, concat_axis=2, tiled=True)  187 us
    all_to_all x1, waiting for transfers between devices, body(): lax.all_to_all(result.reshape(2, groups, own_cols, own_rows), 'rows', spl...  175 us
    unnamed x17, local copies, waits for them, and re-layouts  73.8 us
    transpose x3, local copies, waits for them, and re-layouts, contract(): jnp.einsum(form, left, right, precision=lax.Precision.HIGHEST, preferred_...  50.5 us
    another operation x2, local copies, waits for them, and re-layouts, along_last(): stacked.reshape(2, lead, P_SIZE, Q)  34.8 us
  transfers between devices with their start and end apart: 2, of which 2 were waited for; matrix products, arithmetic and copies ran while one was open for 1% of the time, Pallas kernels for 0%

commit v1 on v0

--- a/solution.py
+++ b/solution.py
@@ -2,7 +2,11 @@
 
 import jax
 import jax.numpy as jnp
+import ml_dtypes
+import numpy as np
 from jax import lax
+from jax.experimental import pallas as pl
+from jax.experimental.pallas import tpu as pltpu
 from jax.sharding import PartitionSpec as P
 
 P_SIZE = 32
@@ -58,7 +62,7 @@
     return contract("cbkq,cqem->ebmk", twisted, second_table).reshape(2, lead, length)
 
 
-def body(object_field, phases, intensity):
+def plain_body(object_field, phases, intensity):
     groups = lax.axis_size("rows")
     masks = lax.axis_size("mask")
     own_rows = object_field.shape[1]
@@ -95,7 +99,632 @@
     return (object_field - step_size * direction, direction)
 
 
+LANES = 128
+
+
+def host_tables(sign, scale):
+    idx = np.arange(Q)
+    angle = sign * 2.0 * np.pi * ((idx[:, None] * idx[None, :]) % Q) / Q
+    cos, sin = np.cos(angle) * scale, np.sin(angle) * scale
+    table = np.block([[cos, sin], [-sin, cos]]).astype(np.float32)
+    high = table.astype(ml_dtypes.bfloat16)
+    low = (table - high.astype(np.float32)).astype(ml_dtypes.bfloat16)
+    return high, low
+
+
+def host_twiddle(sign):
+    expo = np.arange(P_SIZE)[:, None] * np.arange(Q)[None, :]
+    angle = sign * 2.0 * np.pi * expo / (P_SIZE * Q)
+    return np.stack([np.cos(angle), np.sin(angle)]).astype(np.float32)
+
+
+def butterflies(real, imag, sign):
+    count = len(real)
+    if count == 1:
+        return real, imag
+    e_real, e_imag = butterflies(real[0::2], imag[0::2], sign)
+    o_real, o_imag = butterflies(real[1::2], imag[1::2], sign)
+    half = count // 2
+    out_real, out_imag = [None] * count, [None] * count
+    for k in range(half):
+        a, b = o_real[k], o_imag[k]
+        if k == 0:
+            t_real, t_imag = a, b
+        elif 4 * k == count:
+            t_real, t_imag = (b, -a) if sign < 0 else (-b, a)
+        elif 8 * k == count:
+            root = math.sqrt(0.5)
+            if sign < 0:
+                t_real, t_imag = (a + b) * root, (b - a) * root
+            else:
+                t_real, t_imag = (a - b) * root, (a + b) * root
+        elif 8 * k == 3 * count:
+            root = math.sqrt(0.5)
+            if sign < 0:
+                t_real, t_imag = (b - a) * root, (a + b) * -root
+            else:
+                t_real, t_imag = (a + b) * -root, (a - b) * root
+        else:
+            angle = sign * 2.0 * math.pi * k / count
+            c, s = math.cos(angle), math.sin(angle)
+            t_real, t_imag = a * c - b * s, a * s + b * c
+        out_real[k], out_imag[k] = e_real[k] + t_real, e_imag[k] + t_imag
+        out_real[k + half], out_imag[k + half] = e_real[k] - t_real, e_imag[k] - t_imag
+    return out_real, out_imag
+
+
+def halves(value):
+    high = value.astype(jnp.bfloat16)
+    low = (value - high.astype(jnp.float32)).astype(jnp.bfloat16)
+    return high, low
+
+
+def dims_dot(left, right, dims):
+    return lax.dot_general(left, right, (dims, ((), ())), preferred_element_type=jnp.float32)
+
+
+def times_table(value, high_ref, low_ref):
+    high, low = halves(value)
+    dims = ((1,), (0,))
+    total = dims_dot(high, high_ref[...], dims)
+    total += dims_dot(low, high_ref[...], dims)
+    return total + dims_dot(high, low_ref[...], dims)
+
+
+def mask_entry(code):
+    d_real = jnp.where(code == 0, 1.0, 0.0) - jnp.where(code == 2, 1.0, 0.0)
+    d_imag = jnp.where(code == 1, 1.0, 0.0) - jnp.where(code == 3, 1.0, 0.0)
+    return d_real, d_imag
+
+
+def column_block(load, store, power_ref, power_rows, tw_refs, tables, mid_ref, share):
+    twf_ref, twi_ref = tw_refs
+    fh_ref, fl_ref, ih_ref, il_ref = tables
+    for h in range(share // 8):
+        real = [load(0, h, n1) for n1 in range(P_SIZE)]
+        imag = [load(1, h, n1) for n1 in range(P_SIZE)]
+        real, imag = butterflies(real, imag, -1.0)
+        for k1 in range(P_SIZE):
+            c, s = twf_ref[0, k1 : k1 + 1, :], twf_ref[1, k1 : k1 + 1, :]
+            at = slice(k1 * share + h * 8, k1 * share + h * 8 + 8)
+            mid_ref[at, 0:LANES] = real[k1] * c - imag[k1] * s
+            mid_ref[at, LANES : 2 * LANES] = real[k1] * s + imag[k1] * c
+    wave = times_table(mid_ref[...], fh_ref, fl_ref)
+    w_real, w_imag = wave[:, 0:LANES], wave[:, LANES : 2 * LANES]
+    weight = w_real * w_real + w_imag * w_imag - power_ref[power_rows, :]
+    value = jnp.concatenate([w_real * weight, w_imag * weight], axis=1)
+    mid_ref[...] = times_table(value, ih_ref, il_ref)
+    for h in range(share // 8):
+        real, imag = [], []
+        for k1 in range(P_SIZE):
+            c, s = twi_ref[0, k1 : k1 + 1, :], twi_ref[1, k1 : k1 + 1, :]
+            at = slice(k1 * share + h * 8, k1 * share + h * 8 + 8)
+            x, y = mid_ref[at, 0:LANES], mid_ref[at, LANES : 2 * LANES]
+            real.append(x * c - y * s)
+            imag.append(x * s + y * c)
+        real, imag = butterflies(real, imag, 1.0)
+        for n1 in range(P_SIZE):
+            store(0, h, n1, real[n1])
+            store(1, h, n1, imag[n1])
+
+
+MESH = pl.DeviceIdType.MESH
+
+
+def greet(peers):
+    barrier = pltpu.get_barrier_semaphore()
+    for peer in peers:
+        pl.semaphore_signal(barrier, inc=1, device_id=peer, device_id_type=MESH)
+    pl.semaphore_wait(barrier, len(peers))
+
+
+def kernel_forward(
+    z_hbm, code_hbm, power_hbm, twf_ref, twi_ref, ah_ref, al_ref, fh, fl, ih, il,
+    u_hbm, buf, got, z_in, code_in, raw, turned, power, mid_ref,
+    z_sem, code_sem, raw_sem, own_sem, out_sem, send_sem, recv_sem,
+):
+    _, halfs, _, groups, share, _ = buf.shape
+    rows = z_in.shape[2]
+    own = z_hbm.shape[1]
+    batch = P_SIZE // send_sem.shape[0]
+    per = rows // share
+    me = lax.axis_index("rows")
+    peers = [lax.rem(me + d, groups) for d in range(1, groups)]
+
+    def load(i, slot):
+        span = pl.ds(pl.multiple_of(i * rows, rows), rows)
+        return (
+            pltpu.make_async_copy(z_hbm.at[:, span], z_in.at[slot], z_sem.at[slot]),
+            pltpu.make_async_copy(code_hbm.at[0, span], code_in.at[slot], code_sem.at[slot]),
+        )
+
+    def raw_load(o):
+        slot = lax.rem(o, 2)
+        span = pl.ds(pl.multiple_of(o * 8, 8), 8)
+        return pltpu.make_async_copy(power_hbm.at[:, span], raw.at[slot], raw_sem.at[slot])
+
+    octets = P_SIZE // 8
+
+    for copy in load(0, 0):
+        copy.start()
+    raw_load(0).start()
+
+    chunks = own // rows
+
+    def first(i, carry):
+        slot = lax.rem(i, 2)
+
+        @pl.when(i + 1 < chunks)
+        def _():
+            for copy in load(i + 1, lax.rem(i + 1, 2)):
+                copy.start()
+
+        for copy in load(i, slot):
+            copy.wait()
+
+        def eight(g, carry):
+            at = i * per + g // 2
+            h, rest = at // (2 * groups), lax.rem(at, 2 * groups)
+            part, c = rest // groups, lax.rem(rest, groups)
+            sub = pl.ds(pl.multiple_of(lax.rem(g, 2) * 8, 8), 8)
+            span = pl.ds(pl.multiple_of(g * 8, 8), 8)
+            real, imag = [], []
+            for n1 in range(P_SIZE):
+                lanes = pl.ds(n1 * LANES, LANES)
+                d_real, d_imag = mask_entry(code_in[slot, span, lanes])
+                x, y = z_in[slot, 0, span, lanes], z_in[slot, 1, span, lanes]
+                real.append(d_real * x - d_imag * y)
+                imag.append(d_real * y + d_imag * x)
+            real, imag = butterflies(real, imag, -1.0)
+            for k1 in range(P_SIZE):
+                cos, sin = twf_ref[0, k1 : k1 + 1, :], twf_ref[1, k1 : k1 + 1, :]
+                buf[k1, h, part, c, sub, 0:LANES] = real[k1] * cos - imag[k1] * sin
+                buf[k1, h, part, c, sub, LANES : 2 * LANES] = real[k1] * sin + imag[k1] * cos
+            return carry
+
+        return lax.fori_loop(0, rows // 8, eight, carry)
+
+    lax.fori_loop(0, chunks, first, 0)
+    greet([{"rows": peer} for peer in peers])
+
+    def span_of(kg):
+        return pl.ds(kg * batch, batch)
+
+    def permute(o):
+        raw_load(o).wait()
+
+        @pl.when(o + 1 < octets)
+        def _():
+            raw_load(o + 1).start()
+
+        slot = lax.rem(o, 2)
+
+        def turn(i, carry):
+            lanes = pl.ds(pl.multiple_of(i * LANES, LANES), LANES)
+            block = raw[slot, :, :, lanes].reshape(Q, LANES)
+            turned[pl.ds(pl.multiple_of(i * LANES, LANES), LANES), :] = block.T
+            return carry
+
+        lax.fori_loop(0, P_SIZE, turn, 0)
+
+        def back(ak1, carry):
+            block = turned[pl.ds(ak1, Q, stride=P_SIZE), :]
+            power[o, pl.ds(pl.multiple_of(ak1 * Q, Q), Q), :] = block.T
+            return carry
+
+        lax.fori_loop(0, P_SIZE, back, 0)
+
+    def own_copy(kg):
+        span = span_of(kg)
+        return pltpu.make_async_copy(buf.at[span, :, :, me], got.at[me, span], own_sem.at[kg])
+
+    def send(kg, peer, sender):
+        span = span_of(kg)
+        return pltpu.make_async_remote_copy(
+            src_ref=buf.at[span, :, :, peer],
+            dst_ref=got.at[sender, span],
+            send_sem=send_sem.at[kg, peer],
+            recv_sem=recv_sem.at[kg, sender],
+            device_id={"rows": peer},
+            device_id_type=MESH,
+        )
+
+    def spread(kg):
+        def one(j, carry):
+            k1 = kg * batch + j
+            for h in range(halfs):
+                value = buf[k1, h].reshape(2 * Q, 2 * LANES)
+                high, low = halves(value)
+                dims = ((1,), (1,))
+                total = dims_dot(ah_ref[...], high, dims)
+                total += dims_dot(ah_ref[...], low, dims)
+                total += dims_dot(al_ref[...], high, dims)
+                buf[k1, h] = total.reshape(2, groups, share, 2 * LANES)
+            return carry
+
+        lax.fori_loop(0, batch, one, 0)
+        own_copy(kg).start()
+        for peer in peers:
+            send(kg, peer, me).start()
+
+    def gather(kg):
+        own_copy(kg).wait()
+        for peer in peers:
+            send(kg, peer, peer).wait_recv()
+
+        def one(j, carry):
+            k1 = kg * batch + j
+            strided = pl.ds(lax.rem(k1, 8), P_SIZE * share, stride=8)
+            weights = power.at[k1 // 8]
+
+            def where(part, h, n1):
+                s, tile = n1 // (2 * halfs), n1 % (2 * halfs)
+                lanes = pl.ds((tile % 2) * LANES, LANES)
+                return s, k1, tile // 2, part, pl.ds(h * 8, 8), lanes
+
+            def fetch(part, h, n1):
+                return got[where(part, h, n1)]
+
+            def store(part, h, n1, value):
+                got[where(part, h, n1)] = value
+
+            column_block(
+                fetch, store, weights, strided, (twf_ref, twi_ref), (fh, fl, ih, il),
+                mid_ref, share,
+            )
+            return carry
+
+        lax.fori_loop(0, batch, one, 0)
+        out_copy(kg).start()
+
+    def out_copy(kg):
+        span = span_of(kg)
+        return pltpu.make_async_copy(got.at[:, span], u_hbm.at[:, span], out_sem.at[kg])
+
+    count = send_sem.shape[0]
+    lag = 2
+
+    def turn(i, carry):
+        @pl.when(i < count)
+        def _():
+            spread(i)
+
+        @pl.when(jnp.logical_and(i < count, lax.rem(i * batch, 8) == 0))
+        def _():
+            permute(i * batch // 8)
+
+        @pl.when(i >= lag)
+        def _():
+            gather(i - lag)
+
+        return carry
+
+    lax.fori_loop(0, count + lag, turn, 0)
+
+    def finish(kg, carry):
+        out_copy(kg).wait()
+        for peer in peers:
+            send(kg, peer, me).wait_send()
+        return carry
+
+    lax.fori_loop(0, count, finish, 0)
+
+
+def kernel_backward(
+    u_hbm, code_hbm, tw_ref, ih, il,
+    total_hbm, land_a, land_b, buf, term, code_in, slot, stage,
+    code_sem, own_sem, send_sem, recv_sem,
+    a_send, a_recv, b_send, b_recv, s_send, s_recv, o_sem, slot_sem,
+):
+    _, _, _, groups, share, _ = buf.shape
+    quarters = send_sem.shape[0]
+    chunks, _, tall, _ = land_a.shape
+    each = chunks // quarters
+    ring = stage.shape[0]
+    me, z = lax.axis_index("rows"), lax.axis_index("mask")
+    masks = 4
+    peers = [lax.rem(me + d, groups) for d in range(1, groups)]
+    partner = z + 1 - 2 * lax.rem(z, 2)
+    middle = 3 - z
+    inner = jnp.logical_or(z == 1, z == 2)
+    outer = jnp.logical_or(z == 0, z == 3)
+
+    def place(q):
+        return q // 2, pl.ds(pl.multiple_of(lax.rem(q, 2) * LANES, LANES), LANES)
+
+    def own_copy(q):
+        h, lanes = place(q)
+        return pltpu.make_async_copy(
+            u_hbm.at[me, :, h, :, :, lanes], buf.at[:, h, :, me, :, lanes], own_sem.at[q]
+        )
+
+    def send(q, peer, sender):
+        h, lanes = place(q)
+        return pltpu.make_async_remote_copy(
+            src_ref=u_hbm.at[peer, :, h, :, :, lanes],
+            dst_ref=buf.at[:, h, :, sender, :, lanes],
+            send_sem=send_sem.at[q, peer],
+            recv_sem=recv_sem.at[q, sender],
+            device_id={"rows": peer},
+            device_id_type=MESH,
+        )
+
+    def code_load(q):
+        span = pl.ds(pl.multiple_of(q * LANES, LANES), LANES)
+        return pltpu.make_async_copy(code_hbm.at[0, span], code_in.at[lax.rem(q, 2)], code_sem.at[q])
+
+    def start(q):
+        code_load(q).start()
+        own_copy(q).start()
+        for peer in peers:
+            send(q, peer, me).start()
+
+    def sent(q):
+        for peer in peers:
+            send(q, peer, me).wait_send()
+
+    def invert(q):
+        code_load(q).wait()
+        own_copy(q).wait()
+        for peer in peers:
+            send(q, peer, peer).wait_recv()
+        h, lanes = place(q)
+        span = pl.ds(pl.multiple_of(q * LANES, LANES), LANES)
+
+        def one(k1, carry):
+            value = buf[k1, h, :, :, :, lanes].reshape(2 * Q, LANES)
+            total = times_table(value.T, ih, il)
+            cos, sin = tw_ref[0, pl.ds(k1, 1), :], tw_ref[1, pl.ds(k1, 1), :]
+            x, y = total[:, 0:LANES], total[:, LANES : 2 * LANES]
+            term[k1, span, 0:LANES] = x * cos - y * sin
+            term[k1, span, LANES : 2 * LANES] = x * sin + y * cos
+            return carry
+
+        lax.fori_loop(0, P_SIZE, one, 0)
+
+        def eight(g, carry):
+            span = pl.ds(pl.multiple_of(q * LANES + g * 8, 8), 8)
+            near = pl.ds(pl.multiple_of(g * 8, 8), 8)
+            real = [term[k1, span, 0:LANES] for k1 in range(P_SIZE)]
+            imag = [term[k1, span, LANES : 2 * LANES] for k1 in range(P_SIZE)]
+            real, imag = butterflies(real, imag, 1.0)
+            for n1 in range(P_SIZE):
+                code = code_in[lax.rem(q, 2), near, pl.ds(n1 * LANES, LANES)]
+                d_real, d_imag = mask_entry(code)
+                term[n1, span, 0:LANES] = d_real * real[n1] + d_imag * imag[n1]
+                term[n1, span, LANES : 2 * LANES] = d_real * imag[n1] - d_imag * real[n1]
+            return carry
+
+        lax.fori_loop(0, LANES // 8, eight, 0)
+
+    def rows_of(j):
+        return pl.ds(pl.multiple_of(j * tall, tall), tall)
+
+    def hop(j, land, send_sems, recv_sems, target):
+        return pltpu.make_async_remote_copy(
+            src_ref=term.at[:, rows_of(j)],
+            dst_ref=land.at[j],
+            send_sem=send_sems.at[j],
+            recv_sem=recv_sems.at[j],
+            device_id={"mask": target},
+            device_id_type=MESH,
+        )
+
+    def hop_a(j):
+        return hop(j, land_a, a_send, a_recv, partner)
+
+    def hop_b(j):
+        return hop(j, land_b, b_send, b_recv, middle)
+
+    def hop_s(j):
+        return pltpu.make_async_remote_copy(
+            src_ref=stage.at[lax.rem(j, ring)],
+            dst_ref=total_hbm.at[:, rows_of(j)],
+            send_sem=s_send.at[j],
+            recv_sem=s_recv.at[j],
+            device_id={"mask": partner},
+            device_id_type=MESH,
+        )
+
+    def keep(j):
+        return pltpu.make_async_copy(
+            stage.at[lax.rem(j, ring)], total_hbm.at[:, rows_of(j)], o_sem.at[j]
+        )
+
+    def outer_step(j):
+        @pl.when(j >= 2)
+        def _():
+            hop_a(j - 2).wait_send()
+
+        hop_a(j).start()
+
+    def inner_first(j):
+        hop_a(j).wait_recv()
+        copy = pltpu.make_async_copy(land_a.at[j], slot.at[0], slot_sem.at[0])
+        copy.start()
+        copy.wait()
+
+        def add(n1, carry):
+            term[n1, rows_of(j)] = term[n1, rows_of(j)] + slot[0, n1]
+            return carry
+
+        lax.fori_loop(0, P_SIZE, add, 0)
+        hop_b(j).start()
+
+    def inner_second(j):
+        hop_b(j).wait_recv()
+        copy = pltpu.make_async_copy(land_b.at[j], slot.at[1], slot_sem.at[1])
+        copy.start()
+
+        @pl.when(j >= ring)
+        def _():
+            hop_s(j - ring).wait_send()
+            keep(j - ring).wait()
+
+        copy.wait()
+        r = lax.rem(j, ring)
+        for n1 in range(P_SIZE):
+            lanes = pl.ds(n1 * LANES, LANES)
+            total = term[n1, rows_of(j)] + slot[1, n1]
+            stage[r, 0, :, lanes] = total[:, 0:LANES]
+            stage[r, 1, :, lanes] = total[:, LANES : 2 * LANES]
+        hop_s(j).start()
+        keep(j).start()
+
+    greet(
+        [{"rows": peer} for peer in peers]
+        + [{"mask": lax.rem(z + d, masks)} for d in range(1, masks)]
+    )
+    start(0)
+    sent(0)
+    start(1)
+
+    def turn(j, carry):
+        q = j // each
+
+        @pl.when(lax.rem(j, each) == 0)
+        def _():
+            invert(q)
+
+        @pl.when(jnp.logical_and(lax.rem(j, each) == each // 2, q + 2 < quarters))
+        def _():
+            sent(q + 1)
+            start(q + 2)
+
+        @pl.when(outer)
+        def _():
+            outer_step(j)
+
+        @pl.when(inner)
+        def _():
+            inner_first(j)
+
+            @pl.when(j >= 1)
+            def _():
+                inner_second(j - 1)
+
+        return carry
+
+    lax.fori_loop(0, chunks, turn, 0)
+
+    @pl.when(outer)
+    def _():
+        hop_a(chunks - 2).wait_send()
+        hop_a(chunks - 1).wait_send()
+
+        def arrive(j, carry):
+            hop_s(j).wait_recv()
+            return carry
+
+        lax.fori_loop(0, chunks, arrive, 0)
+
+    @pl.when(inner)
+    def _():
+        inner_second(chunks - 1)
+
+        def leave(j, carry):
+            hop_b(j).wait_send()
+            return carry
+
+        lax.fori_loop(0, chunks, leave, 0)
+
+        def last(j, carry):
+            hop_s(j).wait_send()
+            keep(j).wait()
+            return carry
+
+        lax.fori_loop(chunks - ring, chunks, last, 0)
+
+    sent(quarters - 1)
+
+
+def fast_body(object_field, phases, intensity):
+    groups = lax.axis_size("rows")
+    masks = lax.axis_size("mask")
+    own = object_field.shape[1]
+    length = object_field.shape[2]
+    share = Q // groups
+    half_scale = 1.0 / math.sqrt(length)
+    f_high, f_low = host_tables(-1.0, half_scale)
+    i_high, i_low = host_tables(1.0, half_scale)
+    tw_f, tw_i = host_twiddle(-1.0), host_twiddle(1.0)
+    wide = 2 * Q
+    f32 = jnp.float32
+    vmem = pl.BlockSpec(memory_space=pltpu.VMEM)
+    hbm = pl.BlockSpec(memory_space=pl.ANY)
+    dma = pltpu.SemaphoreType.DMA
+
+    power = intensity[0].reshape(share, P_SIZE, length)
+
+    parts, rows, halfs = 8, 32, own // wide
+    panel = (groups, P_SIZE, halfs, 2, share, wide)
+    u = pl.pallas_call(
+        kernel_forward,
+        in_specs=[hbm] * 3 + [vmem] * 8,
+        out_specs=hbm,
+        out_shape=jax.ShapeDtypeStruct(panel, f32),
+        scratch_shapes=[
+            pltpu.VMEM((P_SIZE, halfs, 2, groups, share, wide), f32),
+            pltpu.VMEM(panel, f32),
+            pltpu.VMEM((2, 2, rows, length), f32),
+            pltpu.VMEM((2, rows, length), jnp.int32),
+            pltpu.VMEM((2, share, 8, length), f32),
+            pltpu.VMEM((length, 8 * share), f32),
+            pltpu.VMEM((P_SIZE // 8, length, Q), f32),
+            pltpu.VMEM((P_SIZE * share, wide), f32),
+            dma((2,)),
+            dma((2,)),
+            dma((2,)),
+            dma((parts,)),
+            dma((parts,)),
+            dma((parts, groups)),
+            dma((parts, groups)),
+        ],
+        compiler_params=pltpu.CompilerParams(
+            collective_id=0, has_side_effects=True, vmem_limit_bytes=58 * 2**20
+        ),
+        name="forward_and_columns",
+    )(object_field, phases, power, tw_f, tw_i, f_high.T, f_low.T, f_high, f_low, i_high, i_low)
+
+    quarters, tall, ring = own // LANES, 16, 4
+    chunks = own // tall
+    landing = jax.ShapeDtypeStruct((chunks, P_SIZE, tall, wide), f32)
+    total, _, _ = pl.pallas_call(
+        kernel_backward,
+        in_specs=[hbm] * 2 + [vmem] * 3,
+        out_specs=[hbm] * 3,
+        out_shape=[jax.ShapeDtypeStruct((2, own, length), f32), landing, landing],
+        scratch_shapes=[
+            pltpu.VMEM((P_SIZE, halfs, 2, groups, share, wide), f32),
+            pltpu.VMEM((P_SIZE, own, wide), f32),
+            pltpu.VMEM((2, LANES, length), jnp.int32),
+            pltpu.VMEM((2, P_SIZE, tall, wide), f32),
+            pltpu.VMEM((ring, 2, tall, length), f32),
+            dma((quarters,)),
+            dma((quarters,)),
+            dma((quarters, groups)),
+            dma((quarters, groups)),
+        ]
+        + [dma((chunks,))] * 7
+        + [dma((2,))],
+        compiler_params=pltpu.CompilerParams(
+            collective_id=1, has_side_effects=True, vmem_limit_bytes=58 * 2**20
+        ),
+        name="back_and_sum",
+    )(u, phases, tw_i, i_high, i_low)
+    direction = total * (1.0 / masks)
+    return (object_field - step_size * direction, direction)
+
+
 def solution(mesh):
+    def body(object_field, phases, intensity):
+        groups = lax.axis_size("rows")
+        masks = lax.axis_size("mask")
+        own, length = object_field.shape[1:]
+        fits = own % LANES == 0 and length == P_SIZE * Q and groups == 8 and masks == 4 and own % 256 == 0
+        run = fast_body if fits else plain_body
+        return run(object_field, phases, intensity)
+
     return jax.shard_map(
         body,
         mesh=mesh,

time: 1620 us -> 703 us (0.43)
  waiting for transfers between devices: 737 us -> 0 us
  Pallas kernels: 0 us -> 677 us
  local copies, waits for them, and re-layouts: 286 us -> 0 us
  matrix products: 221 us -> 0 us
  blocking collectives: 187 us -> 0 us
  other arithmetic: 160 us -> 21.8 us
    pallas_call x0 -> x2, Pallas kernels: none -> 677 us  [the longest x1 468 us: fast_body(): pl.pallas_call(kernel_backward, in_specs=[hbm] * 2 + [vmem] * 3, out_spec...]
    psum x1 -> x0, waiting for transfers between devices: 563 us -> none  [body(): total = lax.psum(term, 'mask')]
    dot_general x8 -> x0, matrix products: 221 us -> none  [contract(): jnp.einsum(form, left, right, precision=lax.Precision.HIGHEST, preferred_...]
    all_to_all x1 -> x0, blocking collectives: 187 us -> none  [body(): lax.all_to_all(outgoing, 'rows', split_axis=2, concat_axis=2, tiled=True)]
    all_to_all x1 -> x0, waiting for transfers between devices: 175 us -> none  [body(): lax.all_to_all(result.reshape(2, groups, own_cols, own_rows), 'rows', spl...]
    transpose x5 -> x0, local copies, waits for them, and re-layouts: 89.3 us -> none  [the longest x3 50.5 us: contract(): jnp.einsum(form, left, right, precision=lax.Precision.HIGHEST, preferred_...]
    unnamed x17 -> x0, local copies, waits for them, and re-layouts: 73.8 us -> none
    another operation x6 -> x0, local copies, waits for them, and re-layouts: 63.7 us -> none  [the longest x2 34.8 us: along_last(): stacked.reshape(2, lead, P_SIZE, Q)]
  transfers between devices with their start and end apart: 2 -> 0, of which waited for: 2 -> 0; matrix products, arithmetic and copies ran while one was open for 1% -> 0% of each run, Pallas kernels for 0% -> 0%
where the time goes in v1:
time: 703 us; the launch traced here: 700 us
  Pallas kernels  677 us (96%)
  other arithmetic  21.8 us (3%)
    pallas_call x1, Pallas kernels, fast_body(): pl.pallas_call(kernel_backward, in_specs=[hbm] * 2 + [vmem] * 3, out_spec...  468 us
    pallas_call x1, Pallas kernels, fast_body(): pl.pallas_call(kernel_forward, in_specs=[hbm] * 3 + [vmem] * 8, out_specs...  209 us
    mul x1, other arithmetic, fast_body(): direction = total * (1.0 / masks)  21.8 us

profile of v1, /device:TPU:0, one launch (start us, length us, event | category | flops | bytes accessed | tf_op | source)
XLA Modules:
  0.0 699.7 jit_solution(12353316772313205879)
XLA Ops:
  0.6 209.1 %forward_and_columns.1.u_hbm = f32[8,32,2,2,16,256]{5,4,3,2,1,0:T(8,128)} custom-call(f32[2,512,4096]{2,1,0:T(8,128)} %z_hbm.1, s32[1,512,4096]{2,1,0:T(8,128)} %code_hbm.3, f32[16,32,4096]{2,1,0:T(8,128)} %bitcast.1, f32[2,32,128]{2,1,0:T(8,128)} %constant.17.clone.twf_ref, f32[2,32,128]{2,1,0:T(8,128)} %constant.18.clone.twi_ref.tw_ref, ...), custom_call_target="tpu_custom_call" | custom-call | tf_op jit(solution)/shard_map/forward_and_columns/pallas_call | solution.py:661
  209.7 468.2 %back_and_sum.1 = (f32[2,512,4096]{2,1,0:T(8,128)}, f32[32,32,16,256]{3,2,1,0:T(8,128)}, f32[32,32,16,256]{3,2,1,0:T(8,128)}) custom-call(f32[8,32,2,2,16,256]{5,4,3,2,1,0:T(8,128)} %forward_and_columns.1.u_hbm, s32[1,512,4096]{2,1,0:T(8,128)} %code_hbm.3, f32[2,32,128]{2,1,0:T(8,128)} %constant.18.clone.twi_ref.tw_ref, ...), custom_call_target="tpu_custom_call" | custom-call | tf_op jit(solution)/shard_map/back_and_sum/pallas_call | solution.py:692
  677.9 21.8 %broadcast_multiply_fusion = (f32[2,512,4096]{2,1,0:T(8,128)}, f32[2,512,4096]{2,1,0:T(8,128)}) fusion(f32[2,512,4096]{2,1,0:T(8,128)} %get-tuple-element.3, f32[2,512,4096]{2,1,0:T(8,128)} %z_hbm.1), kind=kLoop, calls=%fused_computation.1 | loop fusion | flops 12582912 | bytes 67108864 | tf_op jit(solution)/shard_map/mul | solution.py:715

commit v2 on v1

--- a/solution.py
+++ b/solution.py
@@ -382,7 +382,7 @@
         return pltpu.make_async_copy(got.at[:, span], u_hbm.at[:, span], out_sem.at[kg])
 
     count = send_sem.shape[0]
-    lag = 2
+    lag = 3
 
     def turn(i, carry):
         @pl.when(i < count)
@@ -463,11 +463,13 @@
         for peer in peers:
             send(q, peer, me).wait_send()
 
-    def invert(q):
+    def arrived(q):
         code_load(q).wait()
         own_copy(q).wait()
         for peer in peers:
             send(q, peer, peer).wait_recv()
+
+    def invert(q, least, most):
         h, lanes = place(q)
         span = pl.ds(pl.multiple_of(q * LANES, LANES), LANES)
 
@@ -480,8 +482,9 @@
             term[k1, span, LANES : 2 * LANES] = x * sin + y * cos
             return carry
 
-        lax.fori_loop(0, P_SIZE, one, 0)
-
+        lax.fori_loop(least, most, one, 0)
+
+    def finish(q, least, most):
         def eight(g, carry):
             span = pl.ds(pl.multiple_of(q * LANES + g * 8, 8), 8)
             near = pl.ds(pl.multiple_of(g * 8, 8), 8)
@@ -495,7 +498,7 @@
                 term[n1, span, LANES : 2 * LANES] = d_real * imag[n1] - d_imag * real[n1]
             return carry
 
-        lax.fori_loop(0, LANES // 8, eight, 0)
+        lax.fori_loop(least, most, eight, 0)
 
     def rows_of(j):
         return pl.ds(pl.multiple_of(j * tall, tall), tall)
@@ -578,18 +581,15 @@
     start(0)
     sent(0)
     start(1)
+    arrived(0)
+    invert(0, 0, P_SIZE)
+    finish(0, 0, LANES // 8)
+    half = each // 2
+    lines, groups8 = P_SIZE // 2, LANES // 16
 
     def turn(j, carry):
         q = j // each
-
-        @pl.when(lax.rem(j, each) == 0)
-        def _():
-            invert(q)
-
-        @pl.when(jnp.logical_and(lax.rem(j, each) == each // 2, q + 2 < quarters))
-        def _():
-            sent(q + 1)
-            start(q + 2)
+        step = lax.rem(j, each) - half
 
         @pl.when(outer)
         def _():
@@ -602,6 +602,23 @@
             @pl.when(j >= 1)
             def _():
                 inner_second(j - 1)
+
+        @pl.when(jnp.logical_and(step == 0, q + 1 < quarters))
+        def _():
+            arrived(q + 1)
+
+            @pl.when(q + 2 < quarters)
+            def _():
+                sent(q + 1)
+                start(q + 2)
+
+        @pl.when(jnp.logical_and(jnp.logical_and(step >= 0, step < 2), q + 1 < quarters))
+        def _():
+            invert(q + 1, step * lines, step * lines + lines)
+
+        @pl.when(jnp.logical_and(step >= 2, q + 1 < quarters))
+        def _():
+            finish(q + 1, (step - 2) * groups8, (step - 1) * groups8)
 
         return carry
 
@@ -656,7 +673,7 @@
 
     power = intensity[0].reshape(share, P_SIZE, length)
 
-    parts, rows, halfs = 8, 32, own // wide
+    parts, rows, halfs = 16, 32, own // wide
     panel = (groups, P_SIZE, halfs, 2, share, wide)
     u = pl.pallas_call(
         kernel_forward,

time: 703 us -> 693 us (0.986)
  Pallas kernels: 677 us -> 667 us
    pallas_call x1, Pallas kernels: 468 us -> 457 us  [fast_body(): pl.pallas_call(kernel_backward, in_specs=[hbm] * 2 + [vmem] * 3, out_spec...]
where the time goes in v2:
time: 693 us; the launch traced here: 689 us
  Pallas kernels  667 us (96%)
  other arithmetic  21.8 us (3%)
    pallas_call x1, Pallas kernels, fast_body(): pl.pallas_call(kernel_backward, in_specs=[hbm] * 2 + [vmem] * 3, out_spec...  457 us
    pallas_call x1, Pallas kernels, fast_body(): pl.pallas_call(kernel_forward, in_specs=[hbm] * 3 + [vmem] * 8, out_specs...  210 us
    mul x1, other arithmetic, fast_body(): direction = total * (1.0 / masks)  21.8 us

profile of v2, /device:TPU:0, one launch (start us, length us, event | category | flops | bytes accessed | tf_op | source)
XLA Modules:
  0.0 689.4 jit_solution(16690846963837054317)
XLA Ops:
  0.6 210.0 %forward_and_columns.1.u_hbm = f32[8,32,2,2,16,256]{5,4,3,2,1,0:T(8,128)} custom-call(f32[2,512,4096]{2,1,0:T(8,128)} %z_hbm.1, s32[1,512,4096]{2,1,0:T(8,128)} %code_hbm.3, f32[16,32,4096]{2,1,0:T(8,128)} %bitcast.1, f32[2,32,128]{2,1,0:T(8,128)} %constant.17.clone.twf_ref, f32[2,32,128]{2,1,0:T(8,128)} %constant.18.clone.twi_ref.tw_ref, ...), custom_call_target="tpu_custom_call" | custom-call | tf_op jit(solution)/shard_map/forward_and_columns/pallas_call | solution.py:678
  210.6 457.0 %back_and_sum.1 = (f32[2,512,4096]{2,1,0:T(8,128)}, f32[32,32,16,256]{3,2,1,0:T(8,128)}, f32[32,32,16,256]{3,2,1,0:T(8,128)}) custom-call(f32[8,32,2,2,16,256]{5,4,3,2,1,0:T(8,128)} %forward_and_columns.1.u_hbm, s32[1,512,4096]{2,1,0:T(8,128)} %code_hbm.3, f32[2,32,128]{2,1,0:T(8,128)} %constant.18.clone.twi_ref.tw_ref, ...), custom_call_target="tpu_custom_call" | custom-call | tf_op jit(solution)/shard_map/back_and_sum/pallas_call | solution.py:709
  667.6 21.8 %broadcast_multiply_fusion = (f32[2,512,4096]{2,1,0:T(8,128)}, f32[2,512,4096]{2,1,0:T(8,128)}) fusion(f32[2,512,4096]{2,1,0:T(8,128)} %get-tuple-element.3, f32[2,512,4096]{2,1,0:T(8,128)} %z_hbm.1), kind=kLoop, calls=%fused_computation.1 | loop fusion | flops 12582912 | bytes 67108864 | tf_op jit(solution)/shard_map/mul | solution.py:732

commit v3 on v2

--- a/solution.py
+++ b/solution.py
@@ -585,7 +585,8 @@
     invert(0, 0, P_SIZE)
     finish(0, 0, LANES // 8)
     half = each // 2
-    lines, groups8 = P_SIZE // 2, LANES // 16
+    pieces = half // 2
+    lines, groups8 = P_SIZE // pieces, LANES // 8 // pieces
 
     def turn(j, carry):
         q = j // each
@@ -612,13 +613,13 @@
                 sent(q + 1)
                 start(q + 2)
 
-        @pl.when(jnp.logical_and(jnp.logical_and(step >= 0, step < 2), q + 1 < quarters))
+        @pl.when(jnp.logical_and(jnp.logical_and(step >= 0, step < pieces), q + 1 < quarters))
         def _():
             invert(q + 1, step * lines, step * lines + lines)
 
-        @pl.when(jnp.logical_and(step >= 2, q + 1 < quarters))
-        def _():
-            finish(q + 1, (step - 2) * groups8, (step - 1) * groups8)
+        @pl.when(jnp.logical_and(step >= pieces, q + 1 < quarters))
+        def _():
+            finish(q + 1, (step - pieces) * groups8, (step - pieces + 1) * groups8)
 
         return carry
 
@@ -703,7 +704,7 @@
         name="forward_and_columns",
     )(object_field, phases, power, tw_f, tw_i, f_high.T, f_low.T, f_high, f_low, i_high, i_low)
 
-    quarters, tall, ring = own // LANES, 16, 4
+    quarters, tall, ring = own // LANES, 8, 4
     chunks = own // tall
     landing = jax.ShapeDtypeStruct((chunks, P_SIZE, tall, wide), f32)
     total, _, _ = pl.pallas_call(

time: 693 us -> 685 us (0.988)
  Pallas kernels: 667 us -> 658 us
    pallas_call x1, Pallas kernels: 457 us -> 448 us  [fast_body(): pl.pallas_call(kernel_backward, in_specs=[hbm] * 2 + [vmem] * 3, out_spec...]
where the time goes in v3:
time: 685 us; the launch traced here: 680 us
  Pallas kernels  658 us (96%)
  other arithmetic  21.8 us (3%)
    pallas_call x1, Pallas kernels, fast_body(): pl.pallas_call(kernel_backward, in_specs=[hbm] * 2 + [vmem] * 3, out_spec...  448 us
    pallas_call x1, Pallas kernels, fast_body(): pl.pallas_call(kernel_forward, in_specs=[hbm] * 3 + [vmem] * 8, out_specs...  210 us
    mul x1, other arithmetic, fast_body(): direction = total * (1.0 / masks)  21.8 us

profile of v3, /device:TPU:0, one launch (start us, length us, event | category | flops | bytes accessed | tf_op | source)
XLA Modules:
  0.0 680.4 jit_solution(10421185208765975034)
XLA Ops:
  0.6 210.0 %forward_and_columns.1.u_hbm = f32[8,32,2,2,16,256]{5,4,3,2,1,0:T(8,128)} custom-call(f32[2,512,4096]{2,1,0:T(8,128)} %z_hbm.1, s32[1,512,4096]{2,1,0:T(8,128)} %code_hbm.3, f32[16,32,4096]{2,1,0:T(8,128)} %bitcast.1, f32[2,32,128]{2,1,0:T(8,128)} %constant.17.clone.twf_ref, f32[2,32,128]{2,1,0:T(8,128)} %constant.18.clone.twi_ref.tw_ref, ...), custom_call_target="tpu_custom_call" | custom-call | tf_op jit(solution)/shard_map/forward_and_columns/pallas_call | solution.py:679
  210.6 448.0 %back_and_sum.1 = (f32[2,512,4096]{2,1,0:T(8,128)}, f32[64,32,8,256]{3,2,1,0:T(8,128)}, f32[64,32,8,256]{3,2,1,0:T(8,128)}) custom-call(f32[8,32,2,2,16,256]{5,4,3,2,1,0:T(8,128)} %forward_and_columns.1.u_hbm, s32[1,512,4096]{2,1,0:T(8,128)} %code_hbm.3, f32[2,32,128]{2,1,0:T(8,128)} %constant.18.clone.twi_ref.tw_ref, ...), custom_call_target="tpu_custom_call" | custom-call | tf_op jit(solution)/shard_map/back_and_sum/pallas_call | solution.py:710
  658.6 21.8 %broadcast_multiply_fusion = (f32[2,512,4096]{2,1,0:T(8,128)}, f32[2,512,4096]{2,1,0:T(8,128)}) fusion(f32[2,512,4096]{2,1,0:T(8,128)} %get-tuple-element.3, f32[2,512,4096]{2,1,0:T(8,128)} %z_hbm.1), kind=kLoop, calls=%fused_computation.1 | loop fusion | flops 12582912 | bytes 67108864 | tf_op jit(solution)/shard_map/mul | solution.py:733
